TPU v7x, 32 devices: a whole 2x2x4 slice. The times are simulated.
32 devices in a mesh: fsdp: 32 (over z, y, x, core).
Axes of the slice: x: 2, y: 2, z: 4, core: 2. Of those that a mesh axis runs over, the one named last changes fastest.
Arguments:
- tokens: bfloat16 [12608, 768], P('fsdp'), may hold values from -6 to 6
- ln1_gain: bfloat16 [768], P('fsdp'), may hold values from 0.5 to 1.5
- ln1_shift: bfloat16 [768], P('fsdp'), may hold values from -3 to 3
- qkv_weight: bfloat16 [768, 2304], P('fsdp'), may hold values from -0.21875 to 0.21875
- qv_bias: bfloat16 [2, 768], P(None, 'fsdp'), may hold values from -3 to 3
- proj_weight: bfloat16 [768, 768], P('fsdp'), may hold values from -1 to 1
- proj_bias: bfloat16 [768], P('fsdp'), may hold values from -3 to 3
- ln2_gain: bfloat16 [768], P('fsdp'), may hold values from 0.5 to 1.5
- ln2_shift: bfloat16 [768], P('fsdp'), may hold values from -3 to 3
- router_weight: bfloat16 [768, 4], P('fsdp'), may hold values from -0.15625 to 0.15625
- expert_in: bfloat16 [3072, 4, 768], P('fsdp'), may hold values from -0.21875 to 0.21875
- expert_in_bias: bfloat16 [3072, 4], P('fsdp'), may hold values from -3 to 3
- expert_out: bfloat16 [3072, 4, 768], P('fsdp'), may hold values from -0.3125 to 0.3125
- expert_out_bias: bfloat16 [4, 768], P(None, 'fsdp'), may hold values from -3 to 3
- routes: int32 [12608, 2], P('fsdp'), may hold values from 0 to 3, all different within a row; in each aligned block of 394 rows (0 to 393, 394 to 787, ...) at most 246 rows name the same one
- out_grad: bfloat16 [12608, 768], P('fsdp'), may hold values from -6 to 6
Outputs:
- block_out: bfloat16 [12608, 768], P('fsdp')
- tokens_grad: float32 [12608, 768], P('fsdp')
- ln1_gain_grad: float32 [768], P('fsdp')
- ln1_shift_grad: float32 [768], P('fsdp')
- qkv_weight_grad: float32 [768, 2304], P('fsdp')
- qv_bias_grad: float32 [2, 768], P(None, 'fsdp')
- proj_weight_grad: float32 [768, 768], P('fsdp')
- proj_bias_grad: float32 [768], P('fsdp')
- ln2_gain_grad: float32 [768], P('fsdp')
- ln2_shift_grad: float32 [768], P('fsdp')
- router_weight_grad: float32 [768, 4], P('fsdp')
- expert_in_grad: float32 [3072, 4, 768], P('fsdp')
- expert_in_bias_grad: float32 [3072, 4], P('fsdp')
- expert_out_grad: float32 [3072, 4, 768], P('fsdp')
- expert_out_bias_grad: float32 [4, 768], P(None, 'fsdp')
Inputs may be any that keep to these rules, and one draw needn't show every extreme that they name: `routes`: each row names 2 different experts. Within the rows of one device no expert is named more than 246 times, and in some blocks one expert is named exactly 246 times.
All inputs are finite; a program needn't handle non-finite values.
Results may differ from a plain program's by a relative error of at most 0.015.
Values may be sent and summed in bfloat16 or wider, within the bound.
A program may use at most 320 MiB of HBM per device.

v0:
```python
import jax
import jax.numpy as jnp
from jax import lax
from jax.sharding import PartitionSpec as P

HEADS = 12
HD = 64
EXPERTS = 4
TOP = 2
LEN = 197
SEQ_DEV = 2
CAP = 246


def layer_norm(values, gain_vec, shift_vec):
    row_mean = jnp.mean(values, axis=-1, keepdims=True)
    centred = values - row_mean
    spread = jnp.mean(centred * centred, axis=-1, keepdims=True)
    return centred * lax.rsqrt(spread + 1e-06) * gain_vec + shift_vec


def gelu_tanh(values):
    return jax.nn.gelu(values, approximate=True)


def route_index(routes):
    flat_routes = routes.reshape(-1)
    onehot = (flat_routes[:, None] == jnp.arange(EXPERTS, dtype=jnp.int32)[None, :]).astype(
        jnp.int32
    )
    before = jnp.cumsum(onehot, axis=0) - onehot
    slot_number = jnp.sum(before * onehot, axis=1)
    return flat_routes * CAP + slot_number


def expert_forward(slot_rows, w_in, bias_in, w_out):
    pre_act = (
        jnp.einsum("ecd,fed->ecf", slot_rows, w_in, preferred_element_type=jnp.float32)
        + bias_in.astype(jnp.float32).T[:, None, :]
    )
    hidden = gelu_tanh(pre_act).astype(jnp.bfloat16)
    return jnp.einsum("ecf,fed->ecd", hidden, w_out, preferred_element_type=jnp.float32)


def on_device(
    tokens,
    ln1_gain,
    ln1_shift,
    qkv_weight,
    qv_bias,
    proj_weight,
    proj_bias,
    ln2_gain,
    ln2_shift,
    router_weight,
    expert_in,
    expert_in_bias,
    expert_out,
    expert_out_bias,
    routes,
    out_grad,
):
    highest = lax.Precision.HIGHEST
    row_count = tokens.shape[0]
    model_width = tokens.shape[1]
    slot_count = EXPERTS * CAP
    shape_four = (SEQ_DEV, LEN, HEADS, HD)
    query_scale = HD ** (-0.5)
    gathered = (
        lax.all_gather(ln1_gain, "fsdp", axis=0, tiled=True),
        lax.all_gather(ln1_shift, "fsdp", axis=0, tiled=True),
        lax.all_gather(qkv_weight, "fsdp", axis=0, tiled=True),
        lax.all_gather(qv_bias, "fsdp", axis=1, tiled=True),
        lax.all_gather(proj_weight, "fsdp", axis=0, tiled=True),
        lax.all_gather(proj_bias, "fsdp", axis=0, tiled=True),
        lax.all_gather(ln2_gain, "fsdp", axis=0, tiled=True),
        lax.all_gather(ln2_shift, "fsdp", axis=0, tiled=True),
        lax.all_gather(router_weight, "fsdp", axis=0, tiled=True),
        lax.all_gather(expert_out_bias, "fsdp", axis=1, tiled=True),
    )
    gain1, shift1, w_qkv, bias_qv, w_proj, bias_proj, gain2, shift2, w_router, bias_out = gathered
    inputs = tokens.astype(jnp.float32)
    normed = layer_norm(inputs, gain1.astype(jnp.float32), shift1.astype(jnp.float32)).astype(
        jnp.bfloat16
    )
    projected = jnp.dot(normed, w_qkv, preferred_element_type=jnp.float32)
    bias_qvf = bias_qv.astype(jnp.float32)
    queries = (
        ((projected[:, :model_width] + bias_qvf[0]) * query_scale)
        .astype(jnp.bfloat16)
        .reshape(shape_four)
    )
    key_rows = projected[:, model_width : 2 * model_width].astype(jnp.bfloat16).reshape(shape_four)
    values = (
        (projected[:, 2 * model_width :] + bias_qvf[1]).astype(jnp.bfloat16).reshape(shape_four)
    )
    scores = jnp.einsum("sqhd,skhd->shqk", queries, key_rows, preferred_element_type=jnp.float32)
    top_score = jnp.max(scores, axis=-1, keepdims=True)
    exp_scores = jnp.exp(scores - top_score)
    exp_total = jnp.sum(exp_scores, axis=-1, keepdims=True)
    log_total = top_score + jnp.log(exp_total)
    probs_low = (exp_scores / exp_total).astype(jnp.bfloat16)
    attended = jnp.einsum("shqk,skhd->sqhd", probs_low, values, preferred_element_type=jnp.float32)
    attended = attended.reshape(row_count, model_width).astype(jnp.bfloat16)
    middle = (
        inputs
        + jnp.dot(attended, w_proj, preferred_element_type=jnp.float32)
        + bias_proj.astype(jnp.float32)
    )
    normed2 = layer_norm(middle, gain2.astype(jnp.float32), shift2.astype(jnp.float32)).astype(
        jnp.bfloat16
    )
    gate_probs = jax.nn.softmax(
        jnp.dot(normed2, w_router, preferred_element_type=jnp.float32), axis=-1
    )
    slot_index = route_index(routes)
    onehot = (slot_index[:, None] == jnp.arange(slot_count, dtype=jnp.int32)[None, :]).astype(
        jnp.bfloat16
    )
    onehot = onehot.reshape(row_count, TOP, slot_count)
    picks = (routes[:, :, None] == jnp.arange(EXPERTS, dtype=jnp.int32)[None, None, :]).astype(
        jnp.float32
    )
    chosen = jnp.sum(gate_probs[:, None, :] * picks, axis=2)
    combine = jnp.sum(onehot.astype(jnp.float32) * chosen[:, :, None], axis=1).astype(jnp.bfloat16)
    dispatch = jnp.sum(onehot, axis=1)
    slot_rows = jnp.einsum("tc,td->cd", dispatch, normed2, preferred_element_type=jnp.float32)
    slot_rows = slot_rows.astype(jnp.bfloat16).reshape(EXPERTS, CAP, model_width)
    summed = expert_forward(
        slot_rows,
        lax.all_gather(expert_in, "fsdp", axis=0, tiled=True),
        lax.all_gather(expert_in_bias, "fsdp", axis=0, tiled=True),
        lax.all_gather(expert_out, "fsdp", axis=0, tiled=True),
    )
    result = (summed + bias_out.astype(jnp.float32)[:, None, :]).astype(jnp.bfloat16)
    flat_result = result.reshape(slot_count, model_width)
    block_out = (middle + jnp.dot(combine, flat_result, preferred_element_type=jnp.float32)).astype(
        jnp.bfloat16
    )
    params_back = (
        lax.all_gather(ln1_gain, "fsdp", axis=0, tiled=True),
        lax.all_gather(ln1_shift, "fsdp", axis=0, tiled=True),
        lax.all_gather(qkv_weight, "fsdp", axis=0, tiled=True),
        lax.all_gather(qv_bias, "fsdp", axis=1, tiled=True),
        lax.all_gather(proj_weight, "fsdp", axis=0, tiled=True),
        lax.all_gather(proj_bias, "fsdp", axis=0, tiled=True),
        lax.all_gather(ln2_gain, "fsdp", axis=0, tiled=True),
        lax.all_gather(ln2_shift, "fsdp", axis=0, tiled=True),
        lax.all_gather(router_weight, "fsdp", axis=0, tiled=True),
        lax.all_gather(expert_out_bias, "fsdp", axis=1, tiled=True),
    )
    experts_back = (
        lax.all_gather(expert_in, "fsdp", axis=0, tiled=True),
        lax.all_gather(expert_in_bias, "fsdp", axis=0, tiled=True),
        lax.all_gather(expert_out, "fsdp", axis=0, tiled=True),
    )
    (
        gain1_back,
        shift1_back,
        qkv_back,
        bias_qv_back,
        proj_back,
        bias_proj_back,
        gain2_back,
        shift2_back,
        router_back,
        bias_out_back,
    ) = params_back
    win_back, bias_in_back, wout_back = experts_back
    grad_top = out_grad.astype(jnp.float32)
    grad_result = jnp.einsum("tc,td->cd", combine, out_grad, preferred_element_type=jnp.float32)
    grad_result = grad_result.astype(jnp.bfloat16).reshape(EXPERTS, CAP, model_width)
    routed = jnp.take(flat_result, slot_index, axis=0).reshape(row_count, TOP, model_width)
    grad_chosen = jnp.sum(routed.astype(jnp.float32) * grad_top[:, None, :], axis=2)
    grad_gates = jnp.sum(grad_chosen[:, :, None] * picks, axis=1)
    grad_logits = gate_probs * (
        grad_gates - jnp.sum(gate_probs * grad_gates, axis=-1, keepdims=True)
    )
    grad_router = jnp.dot(normed2.astype(jnp.float32).T, grad_logits, precision=highest)
    grad_normed2 = jnp.dot(grad_logits, router_back.astype(jnp.float32).T, precision=highest)
    pre_act = (
        jnp.einsum("ecd,fed->ecf", slot_rows, win_back, preferred_element_type=jnp.float32)
        + bias_in_back.astype(jnp.float32).T[:, None, :]
    )
    hidden_full, gelu_pull = jax.vjp(gelu_tanh, pre_act)
    hidden = hidden_full.astype(jnp.bfloat16)
    grad_hidden = jnp.einsum(
        "ecd,fed->ecf", grad_result, wout_back, preferred_element_type=jnp.float32
    )
    grad_pre = gelu_pull(grad_hidden)[0].astype(jnp.bfloat16)
    grad_bias_out = jnp.sum(grad_result.astype(jnp.float32), axis=1)
    grad_bias_in = jnp.sum(grad_pre.astype(jnp.float32), axis=1).T
    grad_slots = jnp.einsum("ecf,fed->ecd", grad_pre, win_back, preferred_element_type=jnp.float32)
    grad_slots = grad_slots.astype(jnp.bfloat16).reshape(slot_count, model_width)
    grad_normed2 = grad_normed2 + jnp.dot(dispatch, grad_slots, preferred_element_type=jnp.float32)
    _, norm2_pull = jax.vjp(
        layer_norm, middle, gain2_back.astype(jnp.float32), shift2_back.astype(jnp.float32)
    )
    grad_mid_norm, grad_gain2, grad_shift2 = norm2_pull(grad_normed2)
    grad_middle = grad_top + grad_mid_norm
    grad_branch = grad_middle.astype(jnp.bfloat16)
    grad_bias_proj = jnp.sum(grad_branch.astype(jnp.float32), axis=0)
    grad_proj = jnp.einsum("td,tc->dc", attended, grad_branch, preferred_element_type=jnp.float32)
    grad_attended = jnp.einsum(
        "tc,dc->td", grad_branch, proj_back, preferred_element_type=jnp.float32
    )
    grad_attended = grad_attended.astype(jnp.bfloat16).reshape(shape_four)
    scores_again = jnp.einsum(
        "sqhd,skhd->shqk", queries, key_rows, preferred_element_type=jnp.float32
    )
    probs_full = jnp.exp(scores_again - log_total)
    probs_again = probs_full.astype(jnp.bfloat16)
    grad_probs = jnp.einsum(
        "sqhd,skhd->shqk", grad_attended, values, preferred_element_type=jnp.float32
    )
    grad_values = jnp.einsum(
        "shqk,sqhd->skhd", probs_again, grad_attended, preferred_element_type=jnp.float32
    ).astype(jnp.bfloat16)
    grad_scores = (
        probs_full * (grad_probs - jnp.sum(probs_full * grad_probs, axis=-1, keepdims=True))
    ).astype(jnp.bfloat16)
    grad_queries = jnp.einsum(
        "shqk,skhd->sqhd", grad_scores, key_rows, preferred_element_type=jnp.float32
    ).astype(jnp.bfloat16)
    grad_keys = jnp.einsum(
        "shqk,sqhd->skhd", grad_scores, queries, preferred_element_type=jnp.float32
    ).astype(jnp.bfloat16)
    grad_query_pre = grad_queries.astype(jnp.float32).reshape(row_count, model_width) * query_scale
    grad_values_flat = grad_values.reshape(row_count, model_width)
    grad_projected = jnp.concatenate(
        [
            grad_query_pre.astype(jnp.bfloat16),
            grad_keys.reshape(row_count, model_width),
            grad_values_flat,
        ],
        axis=1,
    )
    grad_bias_qv = jnp.stack(
        [jnp.sum(grad_query_pre, axis=0), jnp.sum(grad_values_flat.astype(jnp.float32), axis=0)]
    )
    grad_qkv_mine = lax.psum_scatter(
        jnp.einsum("td,tc->dc", normed, grad_projected, preferred_element_type=jnp.float32),
        "fsdp",
        scatter_dimension=0,
        tiled=True,
    )
    grad_normed = jnp.einsum(
        "tc,dc->td", grad_projected, qkv_back, preferred_element_type=jnp.float32
    )
    _, norm1_pull = jax.vjp(
        layer_norm, inputs, gain1_back.astype(jnp.float32), shift1_back.astype(jnp.float32)
    )
    grad_in_norm, grad_gain1, grad_shift1 = norm1_pull(grad_normed)
    tokens_grad = grad_middle + grad_in_norm
    term_in = jnp.einsum("ecd,ecf->fed", slot_rows, grad_pre, preferred_element_type=jnp.float32)
    term_out = jnp.einsum("ecf,ecd->fed", hidden, grad_result, preferred_element_type=jnp.float32)
    expert_reduced = lax.psum_scatter(
        jnp.concatenate([term_in, term_out], axis=2), "fsdp", scatter_dimension=0, tiled=True
    )
    small = (
        lax.psum_scatter(grad_gain1, "fsdp", scatter_dimension=0, tiled=True),
        lax.psum_scatter(grad_shift1, "fsdp", scatter_dimension=0, tiled=True),
        lax.psum_scatter(grad_bias_qv, "fsdp", scatter_dimension=1, tiled=True),
        lax.psum_scatter(grad_proj, "fsdp", scatter_dimension=0, tiled=True),
        lax.psum_scatter(grad_bias_proj, "fsdp", scatter_dimension=0, tiled=True),
        lax.psum_scatter(grad_gain2, "fsdp", scatter_dimension=0, tiled=True),
        lax.psum_scatter(grad_shift2, "fsdp", scatter_dimension=0, tiled=True),
        lax.psum_scatter(grad_router, "fsdp", scatter_dimension=0, tiled=True),
        lax.psum_scatter(grad_bias_in, "fsdp", scatter_dimension=0, tiled=True),
        lax.psum_scatter(grad_bias_out, "fsdp", scatter_dimension=1, tiled=True),
    )
    expert_in_grad = expert_reduced[:, :, :model_width]
    expert_out_grad = expert_reduced[:, :, model_width:]
    return (
        block_out,
        tokens_grad,
        small[0],
        small[1],
        grad_qkv_mine,
        small[2],
        small[3],
        small[4],
        small[5],
        small[6],
        small[7],
        expert_in_grad,
        small[8],
        expert_out_grad,
        small[9],
    )


def solution(mesh):
    in_specs = (
        P("fsdp", None),
        P("fsdp"),
        P("fsdp"),
        P("fsdp", None),
        P(None, "fsdp"),
        P("fsdp", None),
        P("fsdp"),
        P("fsdp"),
        P("fsdp"),
        P("fsdp", None),
        P("fsdp", None, None),
        P("fsdp", None),
        P("fsdp", None, None),
        P(None, "fsdp"),
        P("fsdp", None),
        P("fsdp", None),
    )
    out_specs = (
        P("fsdp", None),
        P("fsdp", None),
        P("fsdp"),
        P("fsdp"),
        P("fsdp", None),
        P(None, "fsdp"),
        P("fsdp", None),
        P("fsdp"),
        P("fsdp"),
        P("fsdp"),
        P("fsdp", None),
        P("fsdp", None, None),
        P("fsdp", None),
        P("fsdp", None, None),
        P(None, "fsdp"),
    )
    return jax.shard_map(
        on_device, mesh=mesh, in_specs=in_specs, out_specs=out_specs, check_vma=False
    )
```

profile of v0, /device:TPU:0, one launch (start us, length us, event | category | flops | bytes accessed | tf_op | source)
XLA Modules:
  0.0 1918.3 jit_solution(17703011228541117325)
XLA Ops:
  8.8 2.0 copy.158
  10.9 2.0 copy.160
  14.1 42.2 %all-reduce.16 = (bf16[768]{0:T(1024)(128)(2,1)S(1)}, bf16[768]{0:T(1024)(128)(2,1)S(1)}, bf16[768]{0:T(1024)(128)(2,1)S(1)}, bf16[768]{0:T(1024)(128)(2,1)S(1)}, bf16[768]{0:T(1024)(128)(2,1)S(1)}) all-reduce(bf16[768]{0:T(1024)(128)(2,1)S(1)} %dynamic-update-slice.1, ...), channel_id=1, replica_groups=mesh['fsdp'=32] {'fsdp'}, use_global_device_ids=true, to_apply=%add.2 | all-reduce | flops 3840 | bytes 15360
  56.4 40.4 %all-gather = bf16[32,24,2]{1,2,0:T(2,128)(2,1)S(1)} all-gather(bf16[1,24,2]{1,2,0:T(2,128)(2,1)S(1)} %bitcast.111), channel_id=1, replica_groups=mesh['fsdp'=32] {'fsdp'}, dimensions={0}, use_global_device_ids=true | all-gather | bytes 3168 | tf_op jit(solution)/shard_map/all_gather | solution.py:73
  97.1 36.7 %all-gather.1 = bf16[32,24,4]{1,2,0:T(4,128)(2,1)S(1)} all-gather(bf16[1,24,4]{1,2,0:T(4,128)(2,1)S(1)} %bitcast.108), channel_id=1, replica_groups=mesh['fsdp'=32] {'fsdp'}, dimensions={0}, use_global_device_ids=true | all-gather | bytes 6336 | tf_op jit(solution)/shard_map/all_gather | solution.py:78
  133.9 38.3 %all-gather.2 = bf16[32,96,4]{1,2,0:T(4,128)(2,1)S(1)} all-gather(bf16[1,96,4]{1,2,0:T(4,128)(2,1)S(1)} %bitcast.109), channel_id=1, replica_groups=mesh['fsdp'=32] {'fsdp'}, dimensions={0}, use_global_device_ids=true | all-gather | bytes 25344 | tf_op jit(solution)/shard_map/all_gather | solution.py:132
  172.3 37.2 %all-gather.3 = bf16[32,24,4]{1,2,0:T(4,128)(2,1)S(1)} all-gather(bf16[1,24,4]{1,2,0:T(4,128)(2,1)S(1)} %bitcast.110), channel_id=1, replica_groups=mesh['fsdp'=32] {'fsdp'}, dimensions={0}, use_global_device_ids=true | all-gather | bytes 6336 | tf_op jit(solution)/shard_map/all_gather | solution.py:79
  210.1 1.1 reduce-window.6
  213.0 3.2 mul.272
  216.8 4.7 fusion.17
  221.6 4.0 fusion.57
  226.5 1.0 fusion.39
  227.5 2.1 reshape.290
  229.6 2.2 copy.149
  231.8 3.3 reshape.291
  235.1 2.2 copy.150
  237.4 3.3 reshape.289
  240.7 3.2 copy.151
  245.5 1.3 copy-done
  247.6 1.1 fusion.29
  249.9 2.3 fusion.66
  253.9 2.1 convolution_convert_fusion.2
  256.0 1.8 reshape.244
  258.2 11.6 fusion.68
  269.8 112.5 %all-gather.15.cloned.1.call-done = bf16[3072,4,768]{2,0,1:T(8,128)(2,1)} async-done(((bf16[96,4,768]{2,0,1:T(8,128)(2,1)}), bf16[3072,4,768]{2,0,1:T(8,128)(2,1)}) %all-gather.15.cloned.1.call-update) | async-done | bytes 18874384 | tf_op jit(solution)/shard_map/all_gather | solution.py:133
  382.3 16.8 add_convert_fusion
  399.0 1.8 reshape.245
  400.8 4.1 gather_fusion
  404.9 2.6 multiply_reduce_fusion.2
  408.6 5.1 multiply_reduce_fusion.1
  414.6 2.1 convolution_convert_fusion.1
  416.6 1.5 reshape.246
  418.2 18.2 convolution_bitcast_fusion
  436.3 18.2 convert_reduce_fusion
  454.5 1.7 copy.185
  456.3 16.8 convolution_bitcast_fusion.1
  473.1 50.1 %pad_maximum_fusion = f32[3072,4,1536]{0,2,1:T(8,128)} fusion(f32[3072,4,768]{0,2,1:T(8,128)} %convolution_bitcast_fusion, f32[3072,4,768]{0,2,1:T(8,128)} %convolution_bitcast_fusion.1), kind=kLoop, calls=%fused_computation.1 | loop fusion | flops 18874368 | bytes 150994944 | tf_op jit(solution)/shard_map/concatenate | solution.py:258
  523.1 88.5 %copy.176 = f32[3072,4,1536]{2,1,0:T(4,128)} copy(f32[3072,4,1536]{0,2,1:T(8,128)} %pad_maximum_fusion) | data formatting | bytes 150994944 | tf_op jit(solution)/shard_map/concatenate | solution.py:258
  612.5 15.5 convolution_convert_fusion
  628.0 1.9 reshape.247
  630.8 2.3 multiply_reduce_fusion.3
  633.7 1.1 copy-done.7
  635.0 2.2 fusion.69
  639.2 1.2 copy.165
  640.5 3.5 convert_reduce_fusion.3
  644.7 1.3 reshape.250
  646.1 3.8 multiply_reduce_fusion
  652.0 1.7 copy.172
  653.7 3.5 reshape.249
  657.2 1.8 fusion.18
  659.9 1.3 convert_element_type.193
  661.2 1.3 constant_dynamic-update-slice_fusion.2
  662.6 1.4 copy-done.31
  664.0 5.3 fusion.55
  669.5 1.2 copy-done.6
  670.9 5.2 fusion.60
  677.8 41.2 %all-reduce.15 = (f32[768]{0:T(1024)S(1)}, f32[768]{0:T(1024)S(1)}, f32[2,768]{1,0:T(2,128)S(1)}, f32[768]{0:T(1024)S(1)}, f32[768]{0:T(1024)S(1)}, /*index=5*/f...) all-reduce(f32[768]{0:T(1024)S(1)} %get-tuple-element.47, ...), channel_id=2, replica_groups=mesh['fsdp'=32] {'fsdp'}, use_global_device_ids=true, to_apply=%region_23.24.clone | all-reduce | flops 11520 | bytes 92160
  723.9 2.9 fusion.27
  726.9 1.6 add_add_fusion.2
  728.5 1.5 copy.186
  729.9 950.8 %all-reduce.19.cloned.1.call-done = f32[3072,4,1536]{2,1,0:T(4,128)} async-done(((f32[3072,4,1536]{2,1,0:T(4,128)}), f32[3072,4,1536]{2,1,0:T(4,128)}) %all-reduce.19.cloned.1.call-update) | async-done | bytes 75497488
  1680.8 3.7 constant_dynamic-slice_fusion.2
  1684.5 101.2 %reduce-scatter.11.cloned.1.call-done = f32[24,768]{1,0:T(8,128)} async-done(((f32[768,768]{1,0:T(8,128)}), f32[24,768]{1,0:T(8,128)}) %reduce-scatter.11.cloned.1.call-update) | async-done | bytes 73744 | tf_op jit(solution)/shard_map/reduce_scatter | solution.py:264
  1785.6 125.4 %reduce-scatter.9.cloned.1.call-done = f32[24,2304]{1,0:T(8,128)} async-done(((f32[768,2304]{1,0:T(8,128)}), f32[24,2304]{1,0:T(8,128)}) %reduce-scatter.9.cloned.1.call-update) | async-done | bytes 221200 | tf_op jit(solution)/shard_map/reduce_scatter | solution.py:241
  (264 shorter events, 29.7 us)
Async XLA Ops:
  7.2 5.8 copy-start.69
  7.2 6.0 copy-start.70
  7.2 6.2 copy-start.71
  7.2 6.5 copy-start.72
  7.2 6.7 copy-start.73
  7.2 49.2 %copy-start.67 = (bf16[2,24]{1,0:T(2,128)(2,1)S(1)}, bf16[2,24]{1,0:T(2,128)(2,1)}, u32[]{:S(2)}) copy-start(bf16[2,24]{1,0:T(2,128)(2,1)} %param.20) | copy-start | bytes 292
  7.2 89.9 %copy-start.64 = (bf16[24,4]{0,1:T(4,128)(2,1)S(1)}, bf16[24,4]{0,1:T(4,128)(2,1)}, u32[]{:S(2)}) copy-start(bf16[24,4]{0,1:T(4,128)(2,1)} %param.25) | copy-start | bytes 580
  7.3 126.6 %copy-start.65 = (bf16[96,4]{0,1:T(4,128)(2,1)S(1)}, bf16[96,4]{0,1:T(4,128)(2,1)}, u32[]{:S(2)}) copy-start(bf16[96,4]{0,1:T(4,128)(2,1)} %param.27) | copy-start | bytes 2308
  7.3 165.0 %copy-start.66 = (bf16[4,24]{1,0:T(4,128)(2,1)S(1)}, bf16[4,24]{1,0:T(4,128)(2,1)}, u32[]{:S(2)}) copy-start(bf16[4,24]{1,0:T(4,128)(2,1)} %param.29) | copy-start | bytes 580
  7.3 202.5 %copy-start.61 = (s32[394,2]{0,1:T(2,128)S(1)}, s32[394,2]{0,1:T(2,128)}, u32[]{:S(2)}) copy-start(s32[394,2]{0,1:T(2,128)} %param.30) | copy-start | bytes 9460
  7.3 214.2 %all-gather.9.cloned.1.call-start = ((), (), s32[]{:S(2)}) async-start(), calls=%async_computation.3 | async-start | bytes 3649536 | tf_op jit(solution)/shard_map/all_gather | solution.py:72
  8.0 241.9 %all-gather.11.cloned.1.call-start = ((), (), s32[]{:S(2)}) async-start(), calls=%async_computation.4 | async-start | bytes 1216512 | tf_op jit(solution)/shard_map/all_gather | solution.py:74
  8.8 249.4 %all-gather.13.cloned.1.call-start = ((), (), s32[]{:S(2)}) async-start(), calls=%async_computation.5 | async-start | bytes 19464192 | tf_op jit(solution)/shard_map/all_gather | solution.py:131
  10.8 201.6 %copy-start.16 = (bf16[394,768]{1,0:T(8,128)(2,1)S(1)}, bf16[394,768]{1,0:T(8,128)(2,1)}, u32[]{:S(2)}) copy-start(bf16[394,768]{1,0:T(8,128)(2,1)} %param.31) | copy-start | bytes 1815556
  10.8 371.5 %all-gather.15.cloned.1.call-start = ((), (), s32[]{:S(2)}) async-start(), calls=%async_computation.6 | async-start | bytes 19464192 | tf_op jit(solution)/shard_map/all_gather | solution.py:133
  12.9 715.6 %reduce-scatter.13.cloned.1.call-start = ((), (), s32[]{:S(2)}) async-start(), calls=%async_computation.9 | async-start | bytes 1622016
  56.4 165.2 %copy-start.62 = (f32[768]{0:T(1024)}, f32[768]{0:T(1024)S(1)}, u32[]{:S(2)}) copy-start(f32[768]{0:T(1024)S(1)} %convert_element_type.159) | copy-start | bytes 9220
  56.4 165.2 %copy-start.45 = (f32[768]{0:T(1024)}, f32[768]{0:T(1024)S(1)}, u32[]{:S(2)}) copy-start(f32[768]{0:T(1024)S(1)} %convert_element_type.158) | copy-start | bytes 9220
  56.4 196.2 %copy-start.39 = (f32[768]{0:T(1024)}, f32[768]{0:T(1024)S(1)}, u32[]{:S(2)}) copy-start(f32[768]{0:T(1024)S(1)} %convert_element_type.172) | copy-start | bytes 9220
  133.9 123.9 %copy-start.41 = (bf16[768,4]{0,1:T(4,128)(2,1)}, bf16[768,4]{0,1:T(4,128)(2,1)S(1)}, u32[]{:S(2)}) copy-start(bf16[768,4]{0,1:T(4,128)(2,1)S(1)} %reshape.273) | copy-start | bytes 18436
  213.0 3.2 copy-start.9
  216.5 9.1 copy-start.47
  216.8 8.8 copy-start.55
  216.8 8.8 copy-start.53
  221.5 32.1 %copy-start.21 = (bf16[394,984]{1,0:T(8,128)(2,1)}, bf16[394,984]{1,0:T(8,128)(2,1)S(1)}, u32[]{:S(2)}) copy-start(bf16[394,984]{1,0:T(8,128)(2,1)S(1)} %fusion.17) | copy-start | bytes 2326180
  231.8 12.0 copy-start.12
  237.3 7.4 copy-start.11
  244.7 2.2 copy-start
  244.7 2.2 copy-start.29
  244.7 2.8 copy-start.24
  249.9 2.4 copy-start.22
  253.9 3.9 copy-start.14
  258.1 11.7 copy-start.37
  258.1 11.7 copy-start.51
  258.1 11.7 copy-start.59
  258.2 149.6 %copy-start.34 = (f32[394,4]{0,1:T(4,128)}, f32[394,4]{0,1:T(4,128)S(1)}, u32[]{:S(2)}) copy-start(f32[394,4]{0,1:T(4,128)S(1)} %fusion.47) | copy-start | bytes 18916
  400.8 4.1 copy-start.1
  456.2 1224.5 %all-reduce.19.cloned.1.call-start = ((), (), s32[]{:S(2)}) async-start(), calls=%async_computation.10 | async-start | bytes 150994944
  611.7 1174.0 %reduce-scatter.11.cloned.1.call-start = ((), (), s32[]{:S(2)}) async-start(), calls=%async_computation.8 | async-start | bytes 2433024 | tf_op jit(solution)/shard_map/reduce_scatter | solution.py:264
  628.0 2.0 copy-start.35
  628.0 2.8 copy-start.4
  628.0 2.8 copy-start.40
  628.0 2.8 copy-start.44
  628.0 2.7 copy-start.50
  630.8 2.3 copy-start.58
  635.0 2.6 copy-start.68
  637.3 1273.7 %reduce-scatter.9.cloned.1.call-start = ((), (), s32[]{:S(2)}) async-start(), calls=%async_computation.7 | async-start | bytes 7299072 | tf_op jit(solution)/shard_map/reduce_scatter | solution.py:241
  643.9 2.2 copy-start.25
  644.7 5.2 slice-start
  646.1 3.8 slice-start.1
  659.0 3.4 copy-start.27
  659.8 2.7 copy-start.26
  661.2 2.8 copy-start.10
  661.2 2.8 copy-start.46
  661.2 2.8 copy-start.48
  661.2 2.8 copy-start.54
  661.2 2.8 copy-start.63
  670.9 5.2 copy-start.56
  670.9 5.2 copy-start.15
  670.9 53.0 %copy-start.5 = (f32[394,768]{1,0:T(8,128)S(1)}, f32[394,768]{1,0:T(8,128)}, u32[]{:S(2)}) copy-start(f32[394,768]{1,0:T(8,128)} %copy-done.3) | copy-start | bytes 3631108
  676.1 47.8 %copy-start.2 = (bf16[984,768]{1,0:T(8,128)(2,1)S(1)}, bf16[984,768]{1,0:T(8,128)(2,1)}, u32[]{:S(2)}) copy-start(bf16[984,768]{1,0:T(8,128)(2,1)} %copy-done.1) | copy-start | bytes 4534276
  723.9 3.0 copy-start.8
  723.9 3.0 copy-start.18
  723.9 3.0 copy-start.20
  (20 other events, 26.5 us)
Sparse Core Ops, SparseCore 0:
  11.0 63.0 all-gather.8
  77.0 52.8 all-gather.10
  132.8 123.7 all-gather.12
  259.4 122.8 all-gather.14
  456.4 95.2 reduce-scatter.12
  611.8 1068.8 all-reduce.18
  1686.6 98.9 reduce-scatter.10
  1792.8 118.1 reduce-scatter.8
where the time goes:
time: 1920 us
  waiting for transfers between devices  1290 us (67%)
  blocking collectives  236 us (12%)
  local copies, waits for them, and re-layouts  163 us (8%)
  matrix products  139 us (7%)
  other arithmetic  71.9 us (4%)
    unnamed x10, waiting for transfers between devices  952 us
    reduce_scatter x1, waiting for transfers between devices, on_device(): lax.psum_scatter(jnp.einsum('td,tc->dc', normed, grad_projected, preferre...  125 us
    all_gather x1, waiting for transfers between devices, on_device(): lax.all_gather(expert_out, 'fsdp', axis=0, tiled=True)  112 us
    reduce_scatter x1, waiting for transfers between devices, on_device(): lax.psum_scatter(grad_proj, 'fsdp', scatter_dimension=0, tiled=True)  101 us
    concatenate x1, local copies, waits for them, and re-layouts, on_device(): jnp.concatenate([term_in, term_out], axis=2)  88.5 us
    unnamed x2, blocking collectives  83.4 us
    concatenate x1, other arithmetic, on_device(): jnp.concatenate([term_in, term_out], axis=2)  50.1 us
    all_gather x1, blocking collectives, on_device(): lax.all_gather(qv_bias, 'fsdp', axis=1, tiled=True)  40.4 us
  transfers between devices with their start and end apart: 8, of which 4 were waited for; matrix products, arithmetic and copies ran while one was open for 15% of the time, Pallas kernels for 0%

commit v1 on v0

v1 whole, which is shorter than its diff:
```python
import functools

import jax
import jax.numpy as jnp
from jax import lax
from jax.sharding import PartitionSpec as P

HEADS = 12
HD = 64
EXPERTS = 4
TOP = 2
LEN = 197
SEQ_DEV = 2
SLOTS = 256
SMALL_ROWS = 8


def layer_norm(values, gain_vec, shift_vec):
    row_mean = jnp.mean(values, axis=-1, keepdims=True)
    centred = values - row_mean
    spread = jnp.mean(centred * centred, axis=-1, keepdims=True)
    return centred * lax.rsqrt(spread + 1e-06) * gain_vec + shift_vec


def gelu_tanh(values):
    return jax.nn.gelu(values, approximate=True)


def take_rows(block, widths):
    pieces, at = [], 0
    for width in widths:
        pieces.append(block[:, at : at + width])
        at += width
    return pieces


def dot_f32(left, right, left_dim, right_dim):
    return lax.dot_general(
        left,
        right,
        (((left_dim,), (right_dim,)), ((), ())),
        preferred_element_type=jnp.float32,
    )


def on_device(
    n_dev,
    tokens,
    ln1_gain,
    ln1_shift,
    qkv_weight,
    qv_bias,
    proj_weight,
    proj_bias,
    ln2_gain,
    ln2_shift,
    router_weight,
    expert_in,
    expert_in_bias,
    expert_out,
    expert_out_bias,
    routes,
    out_grad,
):
    highest = lax.Precision.HIGHEST
    f32 = jnp.float32
    low = jnp.bfloat16
    row_count, model_width = tokens.shape
    shape_four = (SEQ_DEV, LEN, HEADS, HD)
    query_scale = HD ** (-0.5)
    own = qkv_weight.shape[0]
    units = expert_in.shape[0]
    wide = 4 * model_width
    core = lax.axis_index("fsdp") % 2
    same_core = [list(range(c, n_dev, 2)) for c in range(2)]
    swap = [(i, i ^ 1) for i in range(n_dev)]

    small_parts = [
        ln1_gain,
        ln1_shift,
        qv_bias.reshape(-1),
        proj_bias,
        ln2_gain,
        ln2_shift,
        router_weight.T.reshape(-1),
        expert_out_bias.reshape(-1),
        expert_in_bias.T.reshape(-1),
    ]
    small_widths = [p.shape[0] for p in small_parts]
    small_total = sum(small_widths)
    small_mine = jnp.pad(
        jnp.concatenate(small_parts)[None, :], ((0, SMALL_ROWS - 1), (0, wide - small_total))
    )
    dense_mine = jnp.concatenate(
        [jnp.concatenate([qkv_weight, proj_weight], axis=1), small_mine], axis=0
    )
    dense = lax.all_gather(dense_mine, "fsdp", axis=0, tiled=True)
    dense = dense.reshape(n_dev, own + SMALL_ROWS, wide)
    w_in = lax.all_gather(
        expert_in.reshape(units, EXPERTS * model_width),
        "fsdp",
        axis=0,
        tiled=True,
        axis_index_groups=same_core,
    )
    w_out = lax.all_gather(
        expert_out.reshape(units, EXPERTS * model_width),
        "fsdp",
        axis=0,
        tiled=True,
        axis_index_groups=same_core,
    )

    weights = dense[:, :own, :].reshape(n_dev * own, wide)
    w_qkv = weights[:, : 3 * model_width]
    w_proj = weights[:, 3 * model_width :]
    gain1, shift1, bias_qv, bias_proj, gain2, shift2, w_router, bias_out, bias_in = take_rows(
        dense[:, own, :], small_widths
    )
    gain1 = gain1.reshape(-1).astype(f32)
    shift1 = shift1.reshape(-1).astype(f32)
    gain2 = gain2.reshape(-1).astype(f32)
    shift2 = shift2.reshape(-1).astype(f32)
    bias_proj = bias_proj.reshape(-1).astype(f32)
    bias_q = bias_qv[:, :own].reshape(-1).astype(f32)
    bias_v = bias_qv[:, own:].reshape(-1).astype(f32)
    w_router = jnp.stack([p.reshape(-1) for p in take_rows(w_router, [own] * EXPERTS)])
    bias_out = [p.reshape(-1).astype(f32) for p in take_rows(bias_out, [own] * EXPERTS)]
    bias_in = lax.dynamic_index_in_dim(
        bias_in.reshape(n_dev // 2, 2, EXPERTS * units), core, axis=1, keepdims=False
    )
    bias_in = [p.reshape(-1).astype(f32) for p in take_rows(bias_in, [units] * EXPERTS)]

    experts = jnp.arange(EXPERTS, dtype=jnp.int32)[None, :]
    pick = [(routes[:, j : j + 1] == experts).astype(f32) for j in range(TOP)]
    picked = pick[0] + pick[1]
    tri = jnp.arange(row_count)[:, None] > jnp.arange(row_count)[None, :]
    before = dot_f32(tri.astype(low), picked.astype(low), 1, 0)
    slot_ids = jnp.arange(EXPERTS * SLOTS, dtype=jnp.int32)[None, :]
    hit = []
    for j in range(TOP):
        slot = jnp.sum(pick[j] * before, axis=1, keepdims=True).astype(jnp.int32)
        hit.append(slot_ids == routes[:, j : j + 1] * SLOTS + slot)
    dispatch = (hit[0] | hit[1]).astype(low)

    inputs = tokens.astype(f32)
    normed_full, norm1_pull = jax.vjp(layer_norm, inputs, gain1, shift1)
    normed = normed_full.astype(low)
    projected = jnp.dot(normed, w_qkv, preferred_element_type=f32)
    queries = ((projected[:, :model_width] + bias_q) * query_scale).astype(low).reshape(shape_four)
    key_rows = projected[:, model_width : 2 * model_width].astype(low).reshape(shape_four)
    values = (projected[:, 2 * model_width :] + bias_v).astype(low).reshape(shape_four)
    scores = jnp.einsum("sqhd,skhd->shqk", queries, key_rows, preferred_element_type=f32)
    exp_scores = jnp.exp(scores - jnp.max(scores, axis=-1, keepdims=True))
    probs_full = exp_scores / jnp.sum(exp_scores, axis=-1, keepdims=True)
    probs_low = probs_full.astype(low)
    attended = jnp.einsum("shqk,skhd->sqhd", probs_low, values, preferred_element_type=f32)
    attended = attended.reshape(row_count, model_width).astype(low)
    middle = inputs + jnp.dot(attended, w_proj, preferred_element_type=f32) + bias_proj
    normed2_full, norm2_pull = jax.vjp(layer_norm, middle, gain2, shift2)
    normed2 = normed2_full.astype(low)
    gate_probs = jax.nn.softmax(dot_f32(normed2, w_router, 1, 1), axis=-1)
    chosen = [jnp.sum(gate_probs * pick[j], axis=1, keepdims=True) for j in range(TOP)]
    combine = (jnp.where(hit[0], chosen[0], 0.0) + jnp.where(hit[1], chosen[1], 0.0)).astype(low)

    def pair_rows(mine):
        mine = mine.reshape(EXPERTS, SLOTS, model_width)
        theirs = lax.ppermute(mine, "fsdp", swap)
        return [jnp.concatenate([mine[e], theirs[e]], axis=0) for e in range(EXPERTS)]

    def pair_sum(partial):
        sent = jnp.stack([p[SLOTS:].astype(low) for p in partial])
        got = lax.ppermute(sent, "fsdp", swap)
        return [p[:SLOTS] + got[e].astype(f32) for e, p in enumerate(partial)]

    slot_rows = pair_rows(dot_f32(dispatch, normed2, 0, 0).astype(low))
    grad_result_mine = dot_f32(combine, out_grad, 0, 0).astype(low)
    grad_result = pair_rows(grad_result_mine)

    def expert(weight, e):
        return weight[:, e * model_width : (e + 1) * model_width]

    def scatter_units(terms):
        whole = jnp.concatenate([t.astype(low) for t in terms], axis=1)
        return lax.psum_scatter(
            whole, "fsdp", scatter_dimension=0, tiled=True, axis_index_groups=same_core
        )

    each = range(EXPERTS)
    pre_act = [dot_f32(slot_rows[e], expert(w_in, e), 1, 1) + bias_in[e] for e in each]
    hidden, pulls = [], []
    for e in each:
        out, pull = jax.vjp(gelu_tanh, pre_act[e])
        hidden.append(out.astype(low))
        pulls.append(pull)
    expert_out_mine = scatter_units([dot_f32(hidden[e], grad_result[e], 0, 0) for e in each])
    grad_pre = [
        pulls[e](dot_f32(grad_result[e], expert(w_out, e), 1, 1))[0].astype(low) for e in each
    ]
    expert_in_mine = scatter_units([dot_f32(grad_pre[e], slot_rows[e], 0, 0) for e in each])
    grad_bias_in = jnp.stack([jnp.sum(grad_pre[e].astype(f32), axis=0) for e in each])
    summed = pair_sum([dot_f32(hidden[e], expert(w_out, e), 1, 0) for e in each])
    result = jnp.concatenate([(summed[e] + bias_out[e]).astype(low) for e in each], axis=0)
    grad_slots = pair_sum([dot_f32(grad_pre[e], expert(w_in, e), 1, 0) for e in each])
    grad_slots = jnp.concatenate([g.astype(low) for g in grad_slots], axis=0)
    block_out = (middle + jnp.dot(combine, result, preferred_element_type=f32)).astype(low)

    grad_top = out_grad.astype(f32)
    slot_dots = dot_f32(out_grad, result, 1, 1) * dispatch.astype(f32)
    grad_gates = jnp.concatenate(
        [
            jnp.sum(slot_dots[:, e * SLOTS : (e + 1) * SLOTS], axis=1, keepdims=True)
            for e in each
        ],
        axis=1,
    )
    grad_logits = gate_probs * (
        grad_gates - jnp.sum(gate_probs * grad_gates, axis=-1, keepdims=True)
    )
    grad_router = jnp.dot(grad_logits.T, normed2.astype(f32), precision=highest)
    grad_normed2 = jnp.dot(grad_logits, w_router.astype(f32), precision=highest)
    grad_normed2 = grad_normed2 + jnp.dot(dispatch, grad_slots, preferred_element_type=f32)
    grad_mid_norm, grad_gain2, grad_shift2 = norm2_pull(grad_normed2)
    grad_middle = grad_top + grad_mid_norm

    grad_branch = grad_middle.astype(low)
    grad_bias_proj = jnp.sum(grad_branch.astype(f32), axis=0)
    grad_proj = dot_f32(attended, grad_branch, 0, 0)
    grad_attended = dot_f32(grad_branch, w_proj, 1, 1).astype(low).reshape(shape_four)
    grad_probs = jnp.einsum("sqhd,skhd->shqk", grad_attended, values, preferred_element_type=f32)
    grad_values = jnp.einsum(
        "shqk,sqhd->skhd", probs_low, grad_attended, preferred_element_type=f32
    ).astype(low)
    grad_scores = (
        probs_full * (grad_probs - jnp.sum(probs_full * grad_probs, axis=-1, keepdims=True))
    ).astype(low)
    grad_queries = jnp.einsum(
        "shqk,skhd->sqhd", grad_scores, key_rows, preferred_element_type=f32
    ).astype(low)
    grad_keys = jnp.einsum(
        "shqk,sqhd->skhd", grad_scores, queries, preferred_element_type=f32
    ).astype(low)
    grad_query_pre = grad_queries.astype(f32).reshape(row_count, model_width) * query_scale
    grad_values = grad_values.reshape(row_count, model_width)
    grad_projected = jnp.concatenate(
        [grad_query_pre.astype(low), grad_keys.reshape(row_count, model_width), grad_values],
        axis=1,
    )
    grad_qkv = dot_f32(normed, grad_projected, 0, 0)
    grad_normed = dot_f32(grad_projected, w_qkv, 1, 1)
    grad_in_norm, grad_gain1, grad_shift1 = norm1_pull(grad_normed)
    tokens_grad = grad_middle + grad_in_norm

    def by_owner(rows):
        return rows.reshape(-1, n_dev, rows.shape[-1] // n_dev).transpose(1, 0, 2).reshape(n_dev, -1)

    here = (jnp.arange(2) == core).astype(f32)
    bias_in_slots = grad_bias_in.reshape(EXPERTS, n_dev // 2, 1, units) * here[None, None, :, None]
    grad_bias_out = jnp.sum(
        grad_result_mine.astype(f32).reshape(EXPERTS, SLOTS, model_width), axis=1
    )
    small_grads = jnp.concatenate(
        [
            by_owner(
                jnp.concatenate(
                    [
                        jnp.stack(
                            [
                                grad_gain1,
                                grad_shift1,
                                jnp.sum(grad_query_pre, axis=0),
                                jnp.sum(grad_values.astype(f32), axis=0),
                                grad_bias_proj,
                                grad_gain2,
                                grad_shift2,
                            ]
                        ),
                        grad_router,
                        grad_bias_out,
                    ],
                    axis=0,
                )
            ),
            by_owner(bias_in_slots.reshape(EXPERTS, n_dev * units)),
        ],
        axis=1,
    ).astype(low)
    small_grads = jnp.pad(
        small_grads[:, None, :], ((0, 0), (0, SMALL_ROWS - 1), (0, wide - small_total))
    )
    dense_grads = jnp.concatenate([grad_qkv.astype(low), grad_proj.astype(low)], axis=1)
    dense_grads = jnp.concatenate([dense_grads.reshape(n_dev, own, wide), small_grads], axis=1)
    dense_out = lax.psum_scatter(
        dense_grads.reshape(n_dev * (own + SMALL_ROWS), wide),
        "fsdp",
        scatter_dimension=0,
        tiled=True,
    ).astype(f32)
    small = [p[0] for p in take_rows(dense_out[own : own + 1], small_widths)]
    expert_shape = (units, EXPERTS, model_width)
    return (
        block_out,
        tokens_grad,
        small[0],
        small[1],
        dense_out[:own, : 3 * model_width],
        small[2].reshape(2, own),
        dense_out[:own, 3 * model_width :],
        small[3],
        small[4],
        small[5],
        small[6].reshape(EXPERTS, own).T,
        expert_in_mine.astype(f32).reshape(expert_shape),
        small[8].reshape(EXPERTS, units).T,
        expert_out_mine.astype(f32).reshape(expert_shape),
        small[7].reshape(EXPERTS, own),
    )


def solution(mesh):
    in_specs = (
        P("fsdp", None),
        P("fsdp"),
        P("fsdp"),
        P("fsdp", None),
        P(None, "fsdp"),
        P("fsdp", None),
        P("fsdp"),
        P("fsdp"),
        P("fsdp"),
        P("fsdp", None),
        P("fsdp", None, None),
        P("fsdp", None),
        P("fsdp", None, None),
        P(None, "fsdp"),
        P("fsdp", None),
        P("fsdp", None),
    )
    out_specs = (
        P("fsdp", None),
        P("fsdp", None),
        P("fsdp"),
        P("fsdp"),
        P("fsdp", None),
        P(None, "fsdp"),
        P("fsdp", None),
        P("fsdp"),
        P("fsdp"),
        P("fsdp"),
        P("fsdp", None),
        P("fsdp", None, None),
        P("fsdp", None),
        P("fsdp", None, None),
        P(None, "fsdp"),
    )
    return jax.shard_map(
        functools.partial(on_device, mesh.shape["fsdp"]), mesh=mesh, in_specs=in_specs, out_specs=out_specs, check_vma=False
    )
```

time: 1920 us -> 949 us (0.49)
  waiting for transfers between devices: 1290 us -> 671 us
  blocking collectives: 236 us -> 0 us
  local copies, waits for them, and re-layouts: 163 us -> 114 us
  other arithmetic: 71.9 us -> 34.3 us
  matrix products: 139 us -> 104 us
    unnamed x10 -> x8, waiting for transfers between devices: 952 us -> 342 us
    reduce_scatter x2 -> x1, waiting for transfers between devices: 227 us -> 53.9 us  [on_device(): lax.psum_scatter(dense_grads.reshape(n_dev * (own + SMALL_ROWS), wide), '...]
    all_gather x4 -> x3, waiting for transfers between devices: 113 us -> 266 us  [the longest x1 119 us: on_device(): lax.all_gather(expert_out.reshape(units, EXPERTS * model_width), 'fsdp',...]
    all_gather x4 -> x0, blocking collectives: 153 us -> none  [the longest x1 40.4 us: on_device(): lax.all_gather(qv_bias, 'fsdp', axis=1, tiled=True)]
    concatenate x2 -> x14, local copies, waits for them, and re-layouts: 88.6 us -> 4.59 us  [the longest x1 3.42 us: on_device(): jnp.concatenate(small_parts)[None, :]]
    unnamed x2 -> x0, blocking collectives: 83.4 us -> none
    dot_general x22 -> x41, matrix products: 133 us -> 93.8 us  [the longest x33 74.9 us: dot_f32(): lax.dot_general(left, right, (((left_dim,), (right_dim,)), ((), ())), pre...]
    concatenate x1 -> x6, other arithmetic: 50.1 us -> 16.6 us  [the longest x2 8.55 us: scatter_units(): whole = jnp.concatenate([t.astype(low) for t in terms], axis=1)]
  transfers between devices with their start and end apart: 8 -> 10, of which waited for: 4 -> 10; matrix products, arithmetic and copies ran while one was open for 15% -> 13% of each run, Pallas kernels for 0% -> 0%
where the time goes in v1:
time: 949 us; the launch traced here: 941 us
  waiting for transfers between devices  671 us (71%)
  local copies, waits for them, and re-layouts  114 us (12%)
  matrix products  104 us (11%)
  other arithmetic  34.3 us (4%)
  between operations  16 us (2%)
    unnamed x8, waiting for transfers between devices  342 us
    all_gather x1, waiting for transfers between devices, on_device(): lax.all_gather(expert_out.reshape(units, EXPERTS * model_width), 'fsdp',...  119 us
    all_gather x1, waiting for transfers between devices, on_device(): lax.all_gather(expert_in.reshape(units, EXPERTS * model_width), 'fsdp', a...  78.7 us
    dot_general x33, matrix products, dot_f32(): lax.dot_general(left, right, (((left_dim,), (right_dim,)), ((), ())), pre...  74.9 us
    all_gather x1, waiting for transfers between devices, on_device(): dense = lax.all_gather(dense_mine, 'fsdp', axis=0, tiled=True)  68.5 us
    reduce_scatter x1, waiting for transfers between devices, on_device(): lax.psum_scatter(dense_grads.reshape(n_dev * (own + SMALL_ROWS), wide), '...  53.9 us
    unnamed x193, local copies, waits for them, and re-layouts  47.9 us
  transfers between devices with their start and end apart: 10, of which 10 were waited for; matrix products, arithmetic and copies ran while one was open for 13% of the time, Pallas kernels for 0%

profile of v1, /device:TPU:0, one launch (start us, length us, event | category | flops | bytes accessed | tf_op | source)
XLA Modules:
  0.0 941.1 jit_solution(1390603901452545088)
XLA Ops:
  10.4 3.4 concatenate.97
  13.8 1.6 fusion.138
  15.5 2.0 copy.145
  19.3 68.5 %all-gather.4.cloned.1.call-done = bf16[1024,3072]{1,0:T(8,128)(2,1)} async-done(((bf16[32,3072]{1,0:T(8,128)(2,1)}), bf16[1024,3072]{1,0:T(8,128)(2,1)}) %all-gather.4.cloned.1.call-update) | async-done | bytes 6291472 | tf_op jit(solution)/shard_map/all_gather | solution.py:97
  87.8 1.6 slice.418
  89.4 4.8 slice.421
  95.0 3.8 fusion.33
  102.9 3.4 reshape.485
  106.3 2.2 copy.103
  108.5 2.1 reshape.483
  110.6 2.4 copy.104
  113.0 3.8 fusion.180
  116.8 3.0 fusion.90
  121.1 2.4 fusion.181
  124.1 2.5 convolution_convert_fusion.10
  127.4 2.4 fusion.177
  130.3 2.5 slice_bitcast_fusion.15
  132.9 78.7 %all-gather.6.cloned.1.call-done = bf16[1536,3072]{1,0:T(8,128)(2,1)} async-done(((bf16[96,3072]{1,0:T(8,128)(2,1)}), bf16[1536,3072]{1,0:T(8,128)(2,1)}) %all-gather.6.cloned.1.call-update) | async-done | bytes 9437200 | tf_op jit(solution)/shard_map/all_gather | solution.py:99
  211.6 5.0 convolution_add_fusion
  216.5 119.1 %all-gather.8.cloned.1.call-done = bf16[1536,3072]{1,0:T(8,128)(2,1)} async-done(((bf16[96,3072]{1,0:T(8,128)(2,1)}), bf16[1536,3072]{1,0:T(8,128)(2,1)}) %all-gather.8.cloned.1.call-update) | async-done | bytes 9437200 | tf_op jit(solution)/shard_map/all_gather | solution.py:106
  335.7 4.7 fusion.37
  344.4 2.0 fusion.46
  347.5 1.8 convolution_add_fusion.3
  349.4 2.0 fusion.64
  352.9 2.0 fusion.55
  357.7 2.7 collective-permute-done.1
  360.3 2.8 fusion.125
  366.4 3.1 collective-permute-done.2
  369.8 3.5 convert_reduce_fusion.3
  376.4 3.3 convert_reduce_fusion
  382.4 3.3 convert_reduce_fusion.2
  388.4 3.5 convert_reduce_fusion.1
  396.5 2.3 collective-permute-done.3
  398.8 2.7 fusion.117
  405.1 1.8 convolution_convert_fusion.11
  406.9 2.8 convolution_convert_fusion.16
  409.7 3.0 reshape.486
  412.7 2.9 copy.109
  415.6 3.8 fusion.183
  419.4 3.5 multiply_reduce_fusion
  424.1 1.8 fusion.91
  427.4 1.7 copy.119
  429.1 3.4 reshape.444
  432.5 2.8 copy.116
  435.3 3.2 reshape.443
  438.5 2.8 copy.113
  441.4 3.6 convert_element_type.547
  447.5 5.2 fusion.171
  452.7 4.1 convolution_convert_fusion
  457.4 1.9 fusion.95
  460.0 2.9 pad_maximum_fusion.2
  463.0 3.4 fusion.2
  466.6 3.8 convolution_convert_fusion.4
  470.5 1.6 convolution_convert_fusion.1
  475.0 1.6 convolution_convert_fusion.2
  476.6 4.3 pad_maximum_fusion.1
  480.9 12.8 %copy.132 = bf16[1536,3072]{1,0:T(8,128)(2,1)} copy(bf16[1536,3072]{0,1:T(8,128)(2,1)} %pad_maximum_fusion.1) | data formatting | bytes 18874368
  494.0 3.2 convolution_convert_fusion.8
  502.3 4.3 pad_maximum_fusion
  506.5 12.7 %copy.130 = bf16[1536,3072]{1,0:T(8,128)(2,1)} copy(bf16[1536,3072]{0,1:T(8,128)(2,1)} %pad_maximum_fusion) | data formatting | bytes 18874368
  520.3 3.3 fusion.89
  525.2 53.9 %reduce-scatter.8.cloned.1.call-done = bf16[32,3072]{1,0:T(8,128)(2,1)} async-done(((bf16[1024,3072]{1,0:T(8,128)(2,1)}), bf16[32,3072]{1,0:T(8,128)(2,1)}) %reduce-scatter.8.cloned.1.call-update) | async-done | bytes 196624 | tf_op jit(solution)/shard_map/reduce_scatter | solution.py:293
  586.5 169.4 %reduce-scatter.12.cloned.1.call-done = bf16[96,3072]{1,0:T(8,128)(2,1)} async-done(((bf16[1536,3072]{1,0:T(8,128)(2,1)}), bf16[96,3072]{1,0:T(8,128)(2,1)}) %reduce-scatter.12.cloned.1.call-update) | async-done | bytes 589840
  758.7 172.7 %reduce-scatter.10.cloned.1.call-done = bf16[96,3072]{1,0:T(8,128)(2,1)} async-done(((bf16[1536,3072]{1,0:T(8,128)(2,1)}), bf16[96,3072]{1,0:T(8,128)(2,1)}) %reduce-scatter.10.cloned.1.call-update) | async-done | bytes 589840
  (332 shorter events, 71.8 us)
Async XLA Ops:
  7.2 10.4 %copy-start.24 = (bf16[96,4,768]{2,1,0:T(4,128)(2,1)S(1)}, bf16[96,4,768]{2,1,0:T(4,128)(2,1)}, u32[]{:S(2)}) copy-start(bf16[96,4,768]{2,1,0:T(4,128)(2,1)} %param.28) | copy-start | bytes 1769476
  7.2 11.4 %copy-start.56 = (s32[394,2]{0,1:T(2,128)S(1)}, s32[394,2]{0,1:T(2,128)}, u32[]{:S(2)}) copy-start(s32[394,2]{0,1:T(2,128)} %param.30) | copy-start | bytes 9460
  7.2 11.6 %copy-start = (bf16[394,768]{1,0:T(8,128)(2,1)S(1)}, bf16[394,768]{1,0:T(8,128)(2,1)}, u32[]{:S(2)}) copy-start(bf16[394,768]{1,0:T(8,128)(2,1)} %param.16) | copy-start | bytes 1815556
  7.2 80.6 %all-gather.4.cloned.1.call-start = ((), (), s32[]{:S(2)}) async-start(), calls=%async_computation.3 | async-start | bytes 6488064 | tf_op jit(solution)/shard_map/all_gather | solution.py:97
  15.4 196.2 %all-gather.6.cloned.1.call-start = ((), (), s32[]{:S(2)}) async-start(), calls=%async_computation.4 | async-start | bytes 10027008 | tf_op jit(solution)/shard_map/all_gather | solution.py:99
  17.5 318.1 %all-gather.8.cloned.1.call-start = ((), (), s32[]{:S(2)}) async-start(), calls=%async_computation.5 | async-start | bytes 10027008 | tf_op jit(solution)/shard_map/all_gather | solution.py:106
  18.5 560.6 %reduce-scatter.8.cloned.1.call-start = ((), (), s32[]{:S(2)}) async-start(), calls=%async_computation.6 | async-start | bytes 6488064 | tf_op jit(solution)/shard_map/reduce_scatter | solution.py:293
  102.9 10.1 %copy-start.3 = (bf16[2,197,12,64]{1,3,2,0:T(8,128)(2,1)}, bf16[2,197,12,64]{1,3,2,0:T(8,128)(2,1)S(1)}, u32[]{:S(2)}) copy-start(bf16[2,197,12,64]{1,3,2,0:T(8,128)(2,1)S(1)} %copy.102) | copy-start | bytes 1815556
  102.9 5.6 copy-start.7
  108.5 8.4 copy-start.1
  113.0 3.8 copy-start.21
  121.1 2.7 copy-start.19
  126.6 3.8 collective-permute-start
  129.7 210.6 %copy-start.25 = (bf16[256,768]{1,0:T(8,128)(2,1)}, bf16[256,768]{1,0:T(8,128)(2,1)S(1)}, u32[]{:S(2)}) copy-start(bf16[256,768]{1,0:T(8,128)(2,1)S(1)} %get-tuple-element.118) | copy-start | bytes 1179652
  129.7 221.7 %copy-start.27 = (bf16[256,768]{1,0:T(8,128)(2,1)}, bf16[256,768]{1,0:T(8,128)(2,1)S(1)}, u32[]{:S(2)}) copy-start(bf16[256,768]{1,0:T(8,128)(2,1)S(1)} %get-tuple-element.119) | copy-start | bytes 1179652
  335.6 4.7 copy-start.30
  335.6 5.5 copy-start.57
  335.6 7.2 slice-start.5
  335.6 8.4 slice-start.6
  340.4 6.0 copy-start.15
  341.1 3.2 slice-start.7
  344.4 3.2 copy-start.32
  344.4 3.2 copy-start.36
  349.4 2.0 copy-start.33
  351.4 3.5 copy-start.17
  356.6 3.8 collective-permute-start.1
  357.6 5.5 copy-start.8
  363.1 6.6 slice-start.8
  363.1 6.6 slice-start.9
  364.7 5.0 slice-start.10
  366.1 3.5 collective-permute-start.2
  366.4 6.9 copy-start.50
  366.4 10.0 %copy-start.46 = (bf16[256,768]{1,0:T(8,128)(2,1)}, bf16[256,768]{1,0:T(8,128)(2,1)S(1)}, u32[]{:S(2)}) copy-start(bf16[256,768]{1,0:T(8,128)(2,1)S(1)} %get-tuple-element.105) | copy-start | bytes 1179652
  366.4 16.0 %copy-start.44 = (bf16[256,768]{1,0:T(8,128)(2,1)}, bf16[256,768]{1,0:T(8,128)(2,1)S(1)}, u32[]{:S(2)}) copy-start(bf16[256,768]{1,0:T(8,128)(2,1)S(1)} %get-tuple-element.107) | copy-start | bytes 1179652
  366.4 22.0 %copy-start.42 = (bf16[256,768]{1,0:T(8,128)(2,1)}, bf16[256,768]{1,0:T(8,128)(2,1)S(1)}, u32[]{:S(2)}) copy-start(bf16[256,768]{1,0:T(8,128)(2,1)S(1)} %get-tuple-element.106) | copy-start | bytes 1179652
  366.4 3.3 copy-start.74
  369.6 3.7 slice-start.2
  369.7 3.6 copy-start.55
  369.7 6.7 copy-start.53
  369.7 12.7 %copy-start.51 = (bf16[256,768]{1,0:T(8,128)(2,1)}, bf16[256,768]{1,0:T(8,128)(2,1)S(1)}, u32[]{:S(2)}) copy-start(bf16[256,768]{1,0:T(8,128)(2,1)S(1)} %get-tuple-element.111) | copy-start | bytes 1179652
  369.7 18.7 %copy-start.48 = (bf16[256,768]{1,0:T(8,128)(2,1)}, bf16[256,768]{1,0:T(8,128)(2,1)S(1)}, u32[]{:S(2)}) copy-start(bf16[256,768]{1,0:T(8,128)(2,1)S(1)} %get-tuple-element.110) | copy-start | bytes 1179652
  369.8 3.8 slice-start.3
  369.8 4.0 slice-start.4
  373.8 2.6 copy-start.68
  379.8 2.6 copy-start.71
  385.8 2.7 copy-start.66
  395.1 3.8 collective-permute-start.3
  415.6 3.8 copy-start.22
  415.6 3.8 copy-start.23
  415.6 7.3 slice-start
  419.4 3.5 slice-start.1
  445.0 2.5 copy-start.6
  466.4 4.0 copy-start.47
  466.4 289.6 %reduce-scatter.12.cloned.1.call-start = ((), (), s32[]{:S(2)}) async-start(), calls=%async_computation.8 | async-start | bytes 10027008
  466.6 3.8 copy-start.54
  466.6 3.8 copy-start.69
  470.5 2.3 copy-start.72
  472.7 2.3 copy-start.67
  493.8 3.5 copy-start.29
  493.8 437.5 %reduce-scatter.10.cloned.1.call-start = ((), (), s32[]{:S(2)}) async-start(), calls=%async_computation.7 | async-start | bytes 10027008
  494.0 3.3 copy-start.35
  494.0 3.3 copy-start.60
  520.3 3.3 copy-start.5
  520.3 3.3 copy-start.10
  (32 other events, 46.9 us)
Sparse Core Ops, SparseCore 0:
  15.6 72.1 all-gather.3
  90.6 120.9 all-gather.5
  215.0 120.6 all-gather.7
  466.5 112.5 reduce-scatter.7
  585.6 170.3 reduce-scatter.11
  761.5 169.7 reduce-scatter.9

commit v2 on v1

--- a/solution.py
+++ b/solution.py
@@ -181,9 +181,8 @@
         return weight[:, e * model_width : (e + 1) * model_width]
 
     def scatter_units(terms):
-        whole = jnp.concatenate([t.astype(low) for t in terms], axis=1)
         return lax.psum_scatter(
-            whole, "fsdp", scatter_dimension=0, tiled=True, axis_index_groups=same_core
+            terms, "fsdp", scatter_dimension=0, tiled=True, axis_index_groups=same_core
         )
 
     each = range(EXPERTS)
@@ -193,11 +192,18 @@
         out, pull = jax.vjp(gelu_tanh, pre_act[e])
         hidden.append(out.astype(low))
         pulls.append(pull)
-    expert_out_mine = scatter_units([dot_f32(hidden[e], grad_result[e], 0, 0) for e in each])
+    out_terms = [dot_f32(hidden[e], grad_result[e], 0, 0).astype(low) for e in each]
+    out_terms = jnp.concatenate(out_terms, axis=1)
     grad_pre = [
         pulls[e](dot_f32(grad_result[e], expert(w_out, e), 1, 1))[0].astype(low) for e in each
     ]
-    expert_in_mine = scatter_units([dot_f32(grad_pre[e], slot_rows[e], 0, 0) for e in each])
+    in_terms = [dot_f32(grad_pre[e], slot_rows[e], 0, 0).astype(low) for e in each]
+    in_terms = jnp.concatenate(in_terms, axis=1)
+    out_terms, in_terms, hidden, grad_pre = lax.optimization_barrier(
+        (out_terms, in_terms, hidden, grad_pre)
+    )
+    expert_out_mine = scatter_units(out_terms)
+    expert_in_mine = scatter_units(in_terms)
     grad_bias_in = jnp.stack([jnp.sum(grad_pre[e].astype(f32), axis=0) for e in each])
     summed = pair_sum([dot_f32(hidden[e], expert(w_out, e), 1, 0) for e in each])
     result = jnp.concatenate([(summed[e] + bias_out[e]).astype(low) for e in each], axis=0)
@@ -290,6 +296,9 @@
     )
     dense_grads = jnp.concatenate([grad_qkv.astype(low), grad_proj.astype(low)], axis=1)
     dense_grads = jnp.concatenate([dense_grads.reshape(n_dev, own, wide), small_grads], axis=1)
+    dense_grads, expert_out_mine, expert_in_mine = lax.optimization_barrier(
+        (dense_grads, expert_out_mine, expert_in_mine)
+    )
     dense_out = lax.psum_scatter(
         dense_grads.reshape(n_dev * (own + SMALL_ROWS), wide),
         "fsdp",

time: 949 us -> 884 us (0.932)
  waiting for transfers between devices: 671 us -> 595 us
  matrix products: 104 us -> 114 us
    unnamed x8, waiting for transfers between devices: 342 us -> 240 us
    reduce_scatter x1, waiting for transfers between devices: 53.9 us -> 108 us  [on_device(): lax.psum_scatter(dense_grads.reshape(n_dev * (own + SMALL_ROWS), wide), '...]
    all_gather x1, waiting for transfers between devices: 78.7 us -> 65.3 us  [on_device(): lax.all_gather(expert_in.reshape(units, EXPERTS * model_width), 'fsdp', a...]
    dot_general x33, matrix products: 74.9 us -> 87.3 us  [dot_f32(): lax.dot_general(left, right, (((left_dim,), (right_dim,)), ((), ())), pre...]
    unnamed x193 -> x253, local copies, waits for them, and re-layouts: 47.9 us -> 43 us
  transfers between devices with their start and end apart: 10 -> 10, of which waited for: 10 -> 6; matrix products, arithmetic and copies ran while one was open for 13% -> 20% of each run, Pallas kernels for 0% -> 0%
where the time goes in v2:
time: 884 us; the launch traced here: 877 us
  waiting for transfers between devices  595 us (67%)
  local copies, waits for them, and re-layouts  114 us (13%)
  matrix products  114 us (13%)
  other arithmetic  36 us (4%)
  between operations  16.4 us (2%)
    unnamed x8, waiting for transfers between devices  240 us
    all_gather x1, waiting for transfers between devices, on_device(): lax.all_gather(expert_out.reshape(units, EXPERTS * model_width), 'fsdp',...  114 us
    reduce_scatter x1, waiting for transfers between devices, on_device(): lax.psum_scatter(dense_grads.reshape(n_dev * (own + SMALL_ROWS), wide), '...  108 us
    dot_general x33, matrix products, dot_f32(): lax.dot_general(left, right, (((left_dim,), (right_dim,)), ((), ())), pre...  87.3 us
    all_gather x1, waiting for transfers between devices, on_device(): dense = lax.all_gather(dense_mine, 'fsdp', axis=0, tiled=True)  68.1 us
    all_gather x1, waiting for transfers between devices, on_device(): lax.all_gather(expert_in.reshape(units, EXPERTS * model_width), 'fsdp', a...  65.3 us
    unnamed x253, local copies, waits for them, and re-layouts  43 us
  transfers between devices with their start and end apart: 10, of which 6 were waited for; matrix products, arithmetic and copies ran while one was open for 20% of the time, Pallas kernels for 0%

profile of v2, /device:TPU:0, one launch (start us, length us, event | category | flops | bytes accessed | tf_op | source)
XLA Modules:
  0.0 876.5 jit_solution(18161666276513297244)
XLA Ops:
  10.4 3.4 concatenate.97
  13.8 1.6 fusion.138
  15.5 2.0 copy.145
  19.7 68.1 %all-gather.4.cloned.1.call-done = bf16[1024,3072]{1,0:T(8,128)(2,1)} async-done(((bf16[32,3072]{1,0:T(8,128)(2,1)}), bf16[1024,3072]{1,0:T(8,128)(2,1)}) %all-gather.4.cloned.1.call-update) | async-done | bytes 6291472 | tf_op jit(solution)/shard_map/all_gather | solution.py:97
  87.8 1.6 slice.418
  89.4 4.8 slice.421
  99.1 3.8 fusion.33
  107.0 3.4 reshape.485
  110.4 2.2 copy.103
  112.6 2.1 reshape.483
  114.7 2.4 copy.104
  117.1 3.8 fusion.179
  120.9 3.0 fusion.90
  126.0 2.1 fusion.180
  130.1 2.6 bitcast_reduce_fusion
  133.0 2.4 convolution_convert_fusion.10
  136.9 2.4 fusion.177
  139.4 2.4 fusion.176
  141.8 2.6 slice_bitcast_fusion.14
  144.4 2.5 slice_bitcast_fusion.15
  146.9 65.3 %all-gather.6.cloned.1.call-done = bf16[1536,3072]{1,0:T(8,128)(2,1)} async-done(((bf16[96,3072]{1,0:T(8,128)(2,1)}), bf16[1536,3072]{1,0:T(8,128)(2,1)}) %all-gather.6.cloned.1.call-update) | async-done | bytes 9437200 | tf_op jit(solution)/shard_map/all_gather | solution.py:99
  212.2 5.7 multiply_convert_fusion.4
  219.0 2.9 convolution_convert_fusion.8
  221.9 113.8 %all-gather.8.cloned.1.call-done = bf16[1536,3072]{1,0:T(8,128)(2,1)} async-done(((bf16[96,3072]{1,0:T(8,128)(2,1)}), bf16[1536,3072]{1,0:T(8,128)(2,1)}) %all-gather.8.cloned.1.call-update) | async-done | bytes 9437200 | tf_op jit(solution)/shard_map/all_gather | solution.py:106
  335.6 6.2 fusion.9
  343.6 3.7 multiply_convert_fusion.1
  348.9 4.9 fusion.30
  355.5 2.1 multiply_convert_fusion.2
  357.7 1.6 convolution_convert_fusion.6
  359.3 4.6 fusion.23
  365.4 2.2 multiply_convert_fusion.3
  369.0 4.6 fusion.16
  375.9 4.4 pad_maximum_fusion
  380.2 4.3 pad_maximum_fusion.1
  384.5 12.6 %copy.130 = bf16[1536,3072]{1,0:T(8,128)(2,1)} copy(bf16[1536,3072]{0,1:T(8,128)(2,1)} %pad_maximum_fusion) | data formatting | bytes 18874368
  397.2 12.7 %copy.132 = bf16[1536,3072]{1,0:T(8,128)(2,1)} copy(bf16[1536,3072]{0,1:T(8,128)(2,1)} %pad_maximum_fusion.1) | data formatting | bytes 18874368
  411.1 3.7 fusion.53
  414.8 4.2 fusion.47
  426.3 2.6 fusion.68
  428.9 2.6 fusion.62
  431.5 2.5 fusion.59
  436.2 3.6 fusion.65
  439.8 1.9 fusion.133
  444.0 2.9 fusion.125
  449.1 2.7 fusion.117
  457.1 2.0 convolution_convert_fusion.16
  461.2 3.4 fusion.182
  466.8 3.4 multiply_reduce_fusion
  470.3 3.4 multiply_convert_fusion
  474.6 1.7 copy.116
  476.3 3.4 reshape.443
  481.3 2.1 copy.113
  486.2 5.1 fusion.171
  492.7 2.2 convolution_convert_fusion.11
  495.0 2.3 convolution_convert_fusion
  497.9 3.4 fusion.2
  501.3 65.2 %reduce-scatter.10.cloned.1.call-done = bf16[96,3072]{1,0:T(8,128)(2,1)} async-done(((bf16[1536,3072]{1,0:T(8,128)(2,1)}), bf16[96,3072]{1,0:T(8,128)(2,1)}) %reduce-scatter.10.cloned.1.call-update) | async-done | bytes 589840
  566.6 2.2 copy.131
  568.8 174.5 %reduce-scatter.12.cloned.1.call-done = bf16[96,3072]{1,0:T(8,128)(2,1)} async-done(((bf16[1536,3072]{1,0:T(8,128)(2,1)}), bf16[96,3072]{1,0:T(8,128)(2,1)}) %reduce-scatter.12.cloned.1.call-update) | async-done | bytes 589840
  743.3 2.2 copy.133
  746.9 2.8 add_add_fusion.2
  749.8 1.9 fusion.89
  754.2 107.9 %reduce-scatter.8.cloned.1.call-done = bf16[32,3072]{1,0:T(8,128)(2,1)} async-done(((bf16[1024,3072]{1,0:T(8,128)(2,1)}), bf16[32,3072]{1,0:T(8,128)(2,1)}) %reduce-scatter.8.cloned.1.call-update) | async-done | bytes 196624 | tf_op jit(solution)/shard_map/reduce_scatter | solution.py:302
  867.9 1.6 slice.499
  (393 shorter events, 72.0 us)
Async XLA Ops:
  7.2 10.3 %copy-start.37 = (bf16[96,4,768]{2,1,0:T(4,128)(2,1)S(1)}, bf16[96,4,768]{2,1,0:T(4,128)(2,1)}, u32[]{:S(2)}) copy-start(bf16[96,4,768]{2,1,0:T(4,128)(2,1)} %param.28) | copy-start | bytes 1769476
  7.2 11.3 %copy-start.4 = (bf16[394,768]{1,0:T(8,128)(2,1)S(1)}, bf16[394,768]{1,0:T(8,128)(2,1)}, u32[]{:S(2)}) copy-start(bf16[394,768]{1,0:T(8,128)(2,1)} %param.16) | copy-start | bytes 1815556
  7.2 80.6 %all-gather.4.cloned.1.call-start = ((), (), s32[]{:S(2)}) async-start(), calls=%async_computation.3 | async-start | bytes 6488064 | tf_op jit(solution)/shard_map/all_gather | solution.py:97
  15.4 196.7 %all-gather.6.cloned.1.call-start = ((), (), s32[]{:S(2)}) async-start(), calls=%async_computation.4 | async-start | bytes 10027008 | tf_op jit(solution)/shard_map/all_gather | solution.py:99
  15.5 3.6 copy-start.88
  17.5 318.2 %all-gather.8.cloned.1.call-start = ((), (), s32[]{:S(2)}) async-start(), calls=%async_computation.5 | async-start | bytes 10027008 | tf_op jit(solution)/shard_map/all_gather | solution.py:106
  18.5 548.1 %reduce-scatter.10.cloned.1.call-start = ((), (), s32[]{:S(2)}) async-start(), calls=%async_computation.7 | async-start | bytes 10027008
  18.7 80.3 %copy-start.71 = (f32[394]{0:T(512)}, f32[394]{0:T(512)S(1)}, u32[]{:S(2)}) copy-start(f32[394]{0:T(512)S(1)} %broadcast_multiply_fusion.1) | copy-start | bytes 4732
  19.0 75.2 %copy-start.81 = (f32[394]{0:T(512)}, f32[394]{0:T(512)S(1)}, u32[]{:S(2)}) copy-start(f32[394]{0:T(512)S(1)} %fusion.96) | copy-start | bytes 4732
  19.1 80.0 %copy-start.85 = (f32[394]{0:T(512)}, f32[394]{0:T(512)S(1)}, u32[]{:S(2)}) copy-start(f32[394]{0:T(512)S(1)} %fusion.144) | copy-start | bytes 4732
  95.8 33.6 %copy-start.73 = (bf16[1,768]{1,0:T(2,128)(2,1)}, bf16[1,768]{1,0:T(2,128)(2,1)S(1)}, u32[]{:S(2)}) copy-start(bf16[1,768]{1,0:T(2,128)(2,1)S(1)} %stack_reshape.15) | copy-start | bytes 4612
  97.9 5.0 copy-start.67
  98.0 30.5 %copy-start.63 = (f32[768]{0:T(1024)}, f32[768]{0:T(1024)S(1)}, u32[]{:S(2)}) copy-start(f32[768]{0:T(1024)S(1)} %reshape.457) | copy-start | bytes 9220
  98.1 4.8 copy-start.90
  107.0 10.1 %copy-start.8 = (bf16[2,197,12,64]{1,3,2,0:T(8,128)(2,1)}, bf16[2,197,12,64]{1,3,2,0:T(8,128)(2,1)S(1)}, u32[]{:S(2)}) copy-start(bf16[2,197,12,64]{1,3,2,0:T(8,128)(2,1)S(1)} %copy.102) | copy-start | bytes 1815556
  107.0 5.6 copy-start.14
  112.5 8.3 copy-start.6
  117.1 3.8 copy-start.33
  126.0 3.0 copy-start.87
  128.1 326.3 %copy-start = (f32[394,768]{1,0:T(8,128)}, f32[394,768]{1,0:T(8,128)S(1)}, u32[]{:S(2)}) copy-start(f32[394,768]{1,0:T(8,128)S(1)} %get-tuple-element.184) | copy-start | bytes 3631108
  128.2 4.4 copy-start.65
  130.0 321.8 %copy-start.92 = (s32[394,1]{0,1:T(1,128)}, s32[394,1]{0,1:T(1,128)S(1)}, u32[]{:S(2)}) copy-start(s32[394,1]{0,1:T(1,128)S(1)} %get-tuple-element.177) | copy-start | bytes 4732
  130.0 321.8 %copy-start.94 = (s32[394,1]{0,1:T(1,128)}, s32[394,1]{0,1:T(1,128)S(1)}, u32[]{:S(2)}) copy-start(s32[394,1]{0,1:T(1,128)S(1)} %get-tuple-element.178) | copy-start | bytes 4732
  132.6 9.2 %collective-permute-start.1 = (bf16[4,256,768]{2,1,0:T(8,128)(2,1)}, bf16[4,256,768]{2,1,0:T(8,128)(2,1)}, u32[]{:S(2)}, u32[]{:S(2)}) collective-permute-start(bf16[4,256,768]{2,1,0:T(8,128)(2,1)} %bitcast.14), channel_id=1, source_target_pairs={{0,1},{1,0},{2,3},{3,2},{4,5},{5,4},{6,7},{7,6},{8,9},{9,8},{10,11... | collective-permute-start | bytes 4718600 | tf_op jit(solution)/shard_map/ppermute | solution.py:168
  135.4 8.9 %collective-permute-start = (bf16[4,256,768]{2,1,0:T(8,128)(2,1)}, bf16[4,256,768]{2,1,0:T(8,128)(2,1)}, u32[]{:S(2)}, u32[]{:S(2)}) collective-permute-start(bf16[4,256,768]{2,1,0:T(8,128)(2,1)} %bitcast.11), channel_id=1, source_target_pairs={{0,1},{1,0},{2,3},{3,2},{4,5},{5,4},{6,7},{7,6},{8,9},{9,8},{10,11... | collective-permute-start | bytes 4718600 | tf_op jit(solution)/shard_map/ppermute | solution.py:168
  212.2 6.8 copy-start.56
  212.2 6.8 copy-start.58
  335.6 6.3 copy-start.54
  335.6 6.3 copy-start.59
  343.6 3.8 copy-start.52
  343.6 3.8 copy-start.55
  347.4 7.9 slice-start
  348.8 6.5 slice-start.1
  348.9 6.5 slice-start.2
  397.2 346.1 %reduce-scatter.12.cloned.1.call-start = ((), (), s32[]{:S(2)}) async-start(), calls=%async_computation.8 | async-start | bytes 10027008
  409.9 452.1 %reduce-scatter.8.cloned.1.call-start = ((), (), s32[]{:S(2)}) async-start(), calls=%async_computation.6 | async-start | bytes 6488064 | tf_op jit(solution)/shard_map/reduce_scatter | solution.py:302
  411.1 8.1 slice-start.6
  411.1 8.1 slice-start.7
  414.8 4.3 copy-start.27
  414.8 4.4 slice-start.8
  414.8 4.4 copy-start.102
  419.2 5.0 slice-start.3
  419.2 6.2 slice-start.4
  421.2 4.6 slice-start.5
  422.6 3.8 copy-start.24
  424.2 4.7 copy-start.21
  424.2 19.7 %collective-permute-start.2 = (bf16[4,256,768]{2,1,0:T(8,128)(2,1)}, bf16[4,256,768]{2,1,0:T(8,128)(2,1)}, u32[]{:S(2)}, u32[]{:S(2)}) collective-permute-start(bf16[4,256,768]{2,1,0:T(8,128)(2,1)} %pad_maximum_fusion.3), channel_id=1, source_target_pairs={{0,1},{1,0},{2,3},{3,2},{4,5},{5,4},{6,7},{7,6},{8,9},{9,8},{10,11... | collective-permute-start | bytes 4718600 | tf_op jit(solution)/shard_map/ppermute | solution.py:173
  439.7 3.3 copy-start.31
  439.7 3.3 copy-start.19
  439.7 3.3 copy-start.22
  443.0 6.1 collective-permute-start.3
  470.3 3.4 copy-start.9
  474.6 5.1 copy-start.7
  481.3 4.6 copy-start.11
  486.1 5.2 copy-start.60
  486.1 5.2 copy-start.82
  486.2 5.2 copy-start.86
  492.0 2.9 copy-start.91
  746.8 2.9 copy-start.43
  746.8 2.9 copy-start.45
  746.8 2.9 copy-start.93
  746.8 2.9 copy-start.95
  746.9 2.9 copy-start.105
  746.9 2.9 copy-start.107
  (63 other events, 99.1 us)
Sparse Core Ops, SparseCore 0:
  15.5 72.1 all-gather.3
  91.2 120.9 all-gather.5
  215.0 120.6 all-gather.7
  397.3 169.2 reduce-scatter.9
  573.0 170.2 reduce-scatter.11
  748.8 113.1 reduce-scatter.7
